TPU v7x, 32 devices: a whole 2x2x4 slice. The times are simulated.
32 devices in a mesh: dp: 4 (over z), ctx: 2 (over y), exp: 4 (over x, core).
Axes of the slice: x: 2, y: 2, z: 4, core: 2. Of those that a mesh axis runs over, the one named last changes fastest.
Arguments:
- inputs: float32 [4096, 768], P(('dp', 'ctx', 'exp')), may hold values from -6 to 6
- w_query: bfloat16 [2, 768, 768], replicated, may hold values from -0.078125 to 0.078125
- w_key: bfloat16 [2, 768, 768], replicated, may hold values from -0.078125 to 0.078125
- w_value: bfloat16 [2, 768, 768], replicated, may hold values from -0.21875 to 0.21875
- w_out: bfloat16 [2, 768, 768], replicated, may hold values from -1.75 to 1.75
- norm_gain: float32 [4, 768], replicated, may hold values from 0.5 to 1.5
- bias_table: float32 [32, 12], replicated, may hold values from -9 to 9
- dense_in: bfloat16 [768, 3072], replicated, may hold values from -0.21875 to 0.21875
- dense_out: bfloat16 [3072, 768], replicated, may hold values from -0.109375 to 0.109375
- expert_in: bfloat16 [16, 768, 3072], P(('ctx', 'exp')), may hold values from -0.21875 to 0.21875
- expert_out: bfloat16 [16, 3072, 768], P(('ctx', 'exp')), may hold values from -0.21875 to 0.21875
- routes: int32 [4096, 1], P(('dp', 'ctx', 'exp')), may hold values from 0 to 15; in each aligned block of 128 rows (0 to 127, 128 to 255, ...) at most 16 rows name the same one
- gate_scale: float32 [4096, 1], P(('dp', 'ctx', 'exp')), may hold values from 0.45 to 1
- buckets: int32 [2048], replicated, may hold values from 0 to 31, as said below
- cotangent: float32 [4096, 768], P(('dp', 'ctx', 'exp')), may hold values from -6 to 6
Outputs:
- outputs: float32 [4096, 768], P(('dp', 'ctx', 'exp'))
- input_grad: float32 [4096, 768], P(('dp', 'ctx', 'exp'))
- w_query_grad: float32 [2, 768, 768], P(None, None, ('dp', 'ctx', 'exp'))
- w_key_grad: float32 [2, 768, 768], P(None, None, ('dp', 'ctx', 'exp'))
- w_value_grad: float32 [2, 768, 768], P(None, None, ('dp', 'ctx', 'exp'))
- w_out_grad: float32 [2, 768, 768], P(None, None, ('dp', 'ctx', 'exp'))
- norm_gain_grad: float32 [4, 768], P(None, ('dp', 'ctx', 'exp'))
- bias_table_grad: float32 [384], P(('dp', 'ctx', 'exp'))
- dense_in_grad: float32 [768, 3072], P(None, ('dp', 'ctx', 'exp'))
- dense_out_grad: float32 [3072, 768], P(('dp', 'ctx', 'exp'))
- expert_in_grad: float32 [16, 768, 3072], P(('ctx', 'exp'), None, 'dp')
- expert_out_grad: float32 [16, 3072, 768], P(('ctx', 'exp'), 'dp')
Inputs may be any that keep to these rules, and one draw needn't show every extreme that they name: `routes`: at most 16 of the 128 tokens of one device go to one expert. Entry r is the bucket of the distance r - 1024 from a query to a key; distances of zero or less use buckets below 16, and on each side a bucket never falls as the distance moves away from zero.
All inputs are finite; a program needn't handle non-finite values.
Results may differ from a plain program's by a relative error of at most 0.035.
Values may be sent and summed in bfloat16 or wider, within the bound.
A program may use at most 832 MiB of HBM per device.

v0:
```python
import jax
import jax.numpy as jnp
from jax import lax
from jax.sharding import PartitionSpec as P

epsilon = 1e-06
highest = lax.Precision.HIGHEST


def to_half(values):
    return values.astype(jnp.bfloat16)


def widen(values):
    return values.astype(jnp.float32)


def smooth_act(values):
    return values * jax.nn.sigmoid(values)


def smooth_slope(values):
    sigma = jax.nn.sigmoid(values)
    return sigma * (1.0 + values * (1.0 - sigma))


def rms_forward(hidden, gains):
    inv_rms = lax.rsqrt(jnp.mean(hidden * hidden, axis=-1, keepdims=True) + epsilon)
    return (hidden * inv_rms * gains, inv_rms)


def rms_backward(hidden, inv_rms, gains, d_normed):
    d_scaled = d_normed * gains
    d_gains = jnp.sum(d_normed * hidden * inv_rms, axis=0)
    d_hidden = inv_rms * d_scaled - hidden * inv_rms**3 * jnp.mean(
        d_scaled * hidden, axis=-1, keepdims=True
    )
    return (d_hidden, d_gains)


def split_heads(values, head_count):
    return values.reshape(values.shape[0], head_count, values.shape[1] // head_count)


def bias_block(bias_rows, query_first, key_first, query_rows, key_rows, length):
    first_diag = key_first - query_first - (query_rows - 1) + length
    window = lax.dynamic_slice_in_dim(bias_rows, first_diag, query_rows + key_rows - 1, 1)
    offsets = jnp.arange(key_rows)[None, :] - jnp.arange(query_rows)[:, None] + (query_rows - 1)
    return window[:, offsets]


def add_diagonals(d_bias, d_scores, query_first, key_first, length):
    head_count, query_rows, key_rows = d_scores.shape
    diag_count = query_rows + key_rows - 1
    flipped = d_scores[:, ::-1, :]
    padded = jnp.pad(flipped, ((0, 0), (0, 0), (0, query_rows)))
    flattened = padded.reshape(head_count, query_rows * (diag_count + 1))[
        :, : query_rows * diag_count
    ]
    diag_sums = jnp.sum(flattened.reshape(head_count, query_rows, diag_count), axis=1)
    first_diag = key_first - query_first - (query_rows - 1) + length
    return lax.dynamic_update_slice_in_dim(d_bias, diag_sums, first_diag, 1)


def body(
    inputs,
    w_query,
    w_key,
    w_value,
    w_out,
    norm_gain,
    bias_table,
    dense_in,
    dense_out,
    expert_in,
    expert_out,
    routes,
    gate_scale,
    buckets,
    cotangent,
):
    group_rows, model_width = inputs.shape
    head_count = bias_table.shape[1]
    head_size = model_width // head_count
    bucket_count = bias_table.shape[0]
    cycle_size = lax.axis_size(("ctx", "exp"))
    length = group_rows * cycle_size
    my_start = lax.axis_index(("ctx", "exp")) * group_rows
    bucket_picks = (buckets[None, :] == jnp.arange(bucket_count, dtype=jnp.int32)[:, None]).astype(
        jnp.float32
    )
    bias_rows = jnp.dot(bias_table.T, bucket_picks, precision=highest)

    def attention_forward(hidden, gains, weight_query, weight_key, weight_value, weight_out):
        normed, inv_rms = rms_forward(hidden, gains)
        normed_half = to_half(normed)
        queries = to_half(jnp.dot(normed_half, weight_query, preferred_element_type=jnp.float32))
        keys_local = to_half(jnp.dot(normed_half, weight_key, preferred_element_type=jnp.float32))
        values_local = to_half(
            jnp.dot(normed_half, weight_value, preferred_element_type=jnp.float32)
        )
        query_heads = split_heads(queries, head_count)
        row_max = jnp.full((head_count, group_rows), -1e30, jnp.float32)
        weighted = jnp.zeros((group_rows, head_count, head_size), jnp.float32)
        key_piece = lax.all_gather(keys_local, ("ctx", "exp"), axis=0, tiled=True)
        value_piece = lax.all_gather(values_local, ("ctx", "exp"), axis=0, tiled=True)
        key_rows = key_piece.shape[0]
        scores = jnp.einsum(
            "qhd,khd->hqk",
            query_heads,
            split_heads(key_piece, head_count),
            preferred_element_type=jnp.float32,
        )
        scores = scores + bias_block(
            bias_rows, my_start, jnp.int32(0), group_rows, key_rows, length
        )
        new_max = jnp.maximum(row_max, jnp.max(scores, axis=-1))
        rescale = jnp.exp(row_max - new_max)
        weights = jnp.exp(scores - new_max[:, :, None])
        norm_sum = jnp.sum(weights, axis=-1)
        weighted = weighted * rescale.T[:, :, None] + jnp.einsum(
            "hqk,khd->qhd",
            to_half(weights),
            split_heads(value_piece, head_count),
            preferred_element_type=jnp.float32,
        )
        row_max, norm_sum, weighted = (new_max, norm_sum, weighted)
        kept_blocks = (keys_local, values_local)
        log_norm = row_max + jnp.log(norm_sum)
        attended = to_half((weighted / norm_sum.T[:, :, None]).reshape(group_rows, model_width))
        output = hidden + jnp.dot(attended, weight_out, preferred_element_type=jnp.float32)
        return (
            output,
            (
                hidden,
                normed_half,
                inv_rms,
                queries,
                keys_local,
                values_local,
                attended,
                log_norm,
                kept_blocks,
            ),
        )

    def attention_backward(
        layer_cache, grad_out, gains, weight_query, weight_key, weight_value, weight_out
    ):
        (
            hidden,
            normed_half,
            inv_rms,
            queries,
            keys_local,
            values_local,
            attended,
            log_norm,
            kept_blocks,
        ) = layer_cache
        grad_half = to_half(grad_out)
        grad_wout = jnp.dot(attended.T, grad_half, preferred_element_type=jnp.float32)
        d_attended = to_half(jnp.dot(grad_half, weight_out.T, preferred_element_type=jnp.float32))
        query_heads = split_heads(queries, head_count)
        key_heads = split_heads(keys_local, head_count)
        value_heads = split_heads(values_local, head_count)
        grad_heads = split_heads(d_attended, head_count)
        row_delta = jnp.sum(widen(grad_heads) * widen(split_heads(attended, head_count)), axis=-1).T
        norms_all, deltas_all = (
            lax.all_gather(log_norm, ("ctx", "exp"), axis=1, tiled=True),
            lax.all_gather(row_delta, ("ctx", "exp"), axis=1, tiled=True),
        )
        offset = jnp.int32(0)
        d_bias = jnp.zeros(bias_rows.shape, jnp.float32)
        key_piece = lax.all_gather(keys_local, ("ctx", "exp"), axis=0, tiled=True)
        value_piece = lax.all_gather(values_local, ("ctx", "exp"), axis=0, tiled=True)
        key_rows = key_piece.shape[0]
        piece_keys = split_heads(key_piece, head_count)
        scores = jnp.einsum(
            "qhd,khd->hqk", query_heads, piece_keys, preferred_element_type=jnp.float32
        )
        scores = scores + bias_block(bias_rows, my_start, offset, group_rows, key_rows, length)
        weights = jnp.exp(scores - log_norm[:, :, None])
        d_weights = jnp.einsum(
            "qhd,khd->hqk",
            grad_heads,
            split_heads(value_piece, head_count),
            preferred_element_type=jnp.float32,
        )
        d_scores = weights * (d_weights - row_delta[:, :, None])
        d_query = jnp.einsum(
            "hqk,khd->qhd", to_half(d_scores), piece_keys, preferred_element_type=jnp.float32
        )
        d_bias = add_diagonals(d_bias, d_scores, my_start, offset, length)
        d_query, d_bias = (d_query, d_bias)
        query_piece = lax.all_gather(queries, ("ctx", "exp"), axis=0, tiled=True)
        grad_piece = lax.all_gather(d_attended, ("ctx", "exp"), axis=0, tiled=True)
        query_rows = query_piece.shape[0]
        piece_queries = split_heads(query_piece, head_count)
        piece_grads = split_heads(grad_piece, head_count)
        scores = jnp.einsum(
            "qhd,khd->hqk", piece_queries, key_heads, preferred_element_type=jnp.float32
        )
        scores = scores + bias_block(
            bias_rows, jnp.int32(0), my_start, query_rows, group_rows, length
        )
        weights = jnp.exp(scores - norms_all[:, :, None])
        d_weights = jnp.einsum(
            "qhd,khd->hqk", piece_grads, value_heads, preferred_element_type=jnp.float32
        )
        d_scores = weights * (d_weights - deltas_all[:, :, None])
        d_values = jnp.einsum(
            "hqk,qhd->khd", to_half(weights), piece_grads, preferred_element_type=jnp.float32
        )
        d_keys = jnp.einsum(
            "hqk,qhd->khd", to_half(d_scores), piece_queries, preferred_element_type=jnp.float32
        )
        d_keys, d_values = (d_keys, d_values)
        dq_half = to_half(d_query.reshape(group_rows, model_width))
        dk_half = to_half(d_keys.reshape(group_rows, model_width))
        dv_half = to_half(d_values.reshape(group_rows, model_width))
        grad_wq = jnp.dot(normed_half.T, dq_half, preferred_element_type=jnp.float32)
        grad_wk = jnp.dot(normed_half.T, dk_half, preferred_element_type=jnp.float32)
        grad_wv = jnp.dot(normed_half.T, dv_half, preferred_element_type=jnp.float32)
        d_normed = (
            jnp.dot(dq_half, weight_query.T, preferred_element_type=jnp.float32)
            + jnp.dot(dk_half, weight_key.T, preferred_element_type=jnp.float32)
            + jnp.dot(dv_half, weight_value.T, preferred_element_type=jnp.float32)
        )
        d_hidden, d_gains = rms_backward(hidden, inv_rms, gains, d_normed)
        return (grad_out + d_hidden, d_gains, grad_wq, grad_wk, grad_wv, grad_wout, d_bias)

    local_experts = expert_in.shape[0]
    expert_total = local_experts * cycle_size
    capacity = 2 * group_rows // expert_total
    recv_rows = cycle_size * capacity
    flat_routes = routes[:, 0]
    route_hits = (
        flat_routes[:, None] == jnp.arange(expert_total, dtype=jnp.int32)[None, :]
    ).astype(jnp.int32)
    slot_order = jnp.sum((jnp.cumsum(route_hits, axis=0) - 1) * route_hits, axis=1)
    target = flat_routes * capacity + slot_order
    dispatch = (
        target[None, :] == jnp.arange(expert_total * capacity, dtype=jnp.int32)[:, None]
    ).astype(jnp.bfloat16)

    def to_owners(rows_half):
        placed = jnp.dot(dispatch, rows_half, preferred_element_type=jnp.float32)
        return to_half(placed).reshape(cycle_size, local_experts, capacity, model_width)

    def from_owners(returned):
        return jnp.einsum(
            "sc,sd->cd",
            dispatch,
            returned.reshape(expert_total * capacity, model_width),
            preferred_element_type=jnp.float32,
        )

    def expert_backward(layer_cache, grad_out, gains):
        hidden, inv_rms, kept_rows, pre_act, active = layer_cache
        sent_rows = to_owners(to_half(gate_scale * grad_out))
        grad_rows = lax.all_to_all(
            sent_rows, ("ctx", "exp"), split_axis=0, concat_axis=2, tiled=True
        ).reshape(local_experts, recv_rows, model_width)
        grad_eout = jnp.einsum(
            "erf,erd->efd", active, grad_rows, preferred_element_type=jnp.float32
        )
        d_active = jnp.einsum(
            "erd,efd->erf", grad_rows, expert_out, preferred_element_type=jnp.float32
        )
        d_pre = to_half(d_active * smooth_slope(pre_act))
        grad_ein = jnp.einsum("erd,erf->edf", kept_rows, d_pre, preferred_element_type=jnp.float32)
        d_rows = to_half(
            jnp.einsum("erf,edf->erd", d_pre, expert_in, preferred_element_type=jnp.float32)
        )
        returned_grads = lax.all_to_all(
            d_rows.reshape(1, local_experts, recv_rows, model_width),
            ("ctx", "exp"),
            split_axis=2,
            concat_axis=0,
            tiled=True,
        )
        d_normed = from_owners(returned_grads)
        d_hidden, d_gains = rms_backward(hidden, inv_rms, gains, d_normed)
        return (grad_out + d_hidden, d_gains, grad_ein, grad_eout)

    out_one, cache_one = attention_forward(
        inputs, norm_gain[0], w_query[0], w_key[0], w_value[0], w_out[0]
    )
    normed, inv_rms = rms_forward(out_one, norm_gain[1])
    normed_half = to_half(normed)
    pre_act = jnp.dot(normed_half, dense_in, preferred_element_type=jnp.float32)
    active = to_half(smooth_act(pre_act))
    output = out_one + jnp.dot(active, dense_out, preferred_element_type=jnp.float32)
    out_three, cache_three = attention_forward(
        output, norm_gain[2], w_query[1], w_key[1], w_value[1], w_out[1]
    )
    normed, expert_inv_rms = rms_forward(out_three, norm_gain[3])
    expert_normed_half = to_half(normed)
    arrived = lax.all_to_all(
        to_owners(expert_normed_half), ("ctx", "exp"), split_axis=0, concat_axis=2, tiled=True
    ).reshape(local_experts, recv_rows, model_width)
    expert_pre_act = jnp.einsum(
        "erd,edf->erf", arrived, expert_in, preferred_element_type=jnp.float32
    )
    expert_active = to_half(smooth_act(expert_pre_act))
    produced = to_half(
        jnp.einsum("erf,efd->erd", expert_active, expert_out, preferred_element_type=jnp.float32)
    )
    kept_rows = arrived
    returned = lax.all_to_all(
        produced.reshape(1, local_experts, recv_rows, model_width),
        ("ctx", "exp"),
        split_axis=2,
        concat_axis=0,
        tiled=True,
    )
    output = out_three + gate_scale * from_owners(returned)
    cache_four = (out_three, expert_inv_rms, kept_rows, expert_pre_act, expert_active)
    grad_three, gains_four, grad_ein, grad_eout = expert_backward(
        cache_four, cotangent, norm_gain[3]
    )
    grad_two, gains_three, wq_two, wk_two, wv_two, wo_two, bias_two = attention_backward(
        cache_three, grad_three, norm_gain[2], w_query[1], w_key[1], w_value[1], w_out[1]
    )
    hidden, normed_half, inv_rms, pre_act, active = (out_one, normed_half, inv_rms, pre_act, active)
    grad_half = to_half(grad_two)
    grad_dout = jnp.dot(active.T, grad_half, preferred_element_type=jnp.float32)
    d_active = jnp.dot(grad_half, dense_out.T, preferred_element_type=jnp.float32)
    d_pre = to_half(d_active * smooth_slope(pre_act))
    grad_din = jnp.dot(normed_half.T, d_pre, preferred_element_type=jnp.float32)
    d_normed = jnp.dot(d_pre, dense_in.T, preferred_element_type=jnp.float32)
    d_hidden, d_gains = rms_backward(hidden, inv_rms, norm_gain[1], d_normed)
    grad_one, gains_two, grad_din, grad_dout = (grad_two + d_hidden, d_gains, grad_din, grad_dout)
    input_grad, gains_one, wq_one, wk_one, wv_one, wo_one, bias_one = attention_backward(
        cache_one, grad_one, norm_gain[0], w_query[0], w_key[0], w_value[0], w_out[0]
    )
    table_grad = jnp.dot(bucket_picks, (bias_one + bias_two).T, precision=highest).reshape(
        bucket_count * head_count
    )
    shared = (
        lax.psum_scatter(
            jnp.stack([wq_one, wq_two]), ("dp", "ctx", "exp"), scatter_dimension=2, tiled=True
        ),
        lax.psum_scatter(
            jnp.stack([wk_one, wk_two]), ("dp", "ctx", "exp"), scatter_dimension=2, tiled=True
        ),
        lax.psum_scatter(
            jnp.stack([wv_one, wv_two]), ("dp", "ctx", "exp"), scatter_dimension=2, tiled=True
        ),
        lax.psum_scatter(
            jnp.stack([wo_one, wo_two]), ("dp", "ctx", "exp"), scatter_dimension=2, tiled=True
        ),
        lax.psum_scatter(
            jnp.stack([gains_one, gains_two, gains_three, gains_four]),
            ("dp", "ctx", "exp"),
            scatter_dimension=1,
            tiled=True,
        ),
        lax.psum_scatter(table_grad, ("dp", "ctx", "exp"), scatter_dimension=0, tiled=True),
        lax.psum_scatter(grad_din, ("dp", "ctx", "exp"), scatter_dimension=1, tiled=True),
        lax.psum_scatter(grad_dout, ("dp", "ctx", "exp"), scatter_dimension=0, tiled=True),
    )
    expert_sums = (
        lax.psum_scatter(
            grad_ein.astype(jnp.bfloat16), "dp", scatter_dimension=2, tiled=True
        ).astype(jnp.float32),
        lax.psum_scatter(
            grad_eout.astype(jnp.bfloat16), "dp", scatter_dimension=1, tiled=True
        ).astype(jnp.float32),
    )
    return (
        output,
        input_grad,
        shared[0],
        shared[1],
        shared[2],
        shared[3],
        shared[4],
        shared[5],
        shared[6],
        shared[7],
        expert_sums[0],
        expert_sums[1],
    )


def solution(mesh):
    in_specs = (
        P(("dp", "ctx", "exp"), None),
        P(),
        P(),
        P(),
        P(),
        P(),
        P(),
        P(),
        P(),
        P(("ctx", "exp"), None, None),
        P(("ctx", "exp"), None, None),
        P(("dp", "ctx", "exp"), None),
        P(("dp", "ctx", "exp"), None),
        P(),
        P(("dp", "ctx", "exp"), None),
    )
    out_specs = (
        P(("dp", "ctx", "exp"), None),
        P(("dp", "ctx", "exp"), None),
        P(None, None, ("dp", "ctx", "exp")),
        P(None, None, ("dp", "ctx", "exp")),
        P(None, None, ("dp", "ctx", "exp")),
        P(None, None, ("dp", "ctx", "exp")),
        P(None, ("dp", "ctx", "exp")),
        P(("dp", "ctx", "exp")),
        P(None, ("dp", "ctx", "exp")),
        P(("dp", "ctx", "exp"), None),
        P(("ctx", "exp"), None, "dp"),
        P(("ctx", "exp"), "dp", None),
    )
    return jax.shard_map(body, mesh=mesh, in_specs=in_specs, out_specs=out_specs, check_vma=False)
```

profile of v0, /device:TPU:0, one launch (start us, length us, event | category | flops | bytes accessed | tf_op | source)
XLA Modules:
  0.0 2216.1 jit_solution(1764214772100812422)
XLA Ops:
  17.8 433.3 %gather_fusion = f32[131072,12]{1,0:T(8,128)} fusion(f32[12,1151]{0,1:T(8,128)S(1)} %copy.127, s32[131072]{0:T(1024)S(1)} %broadcast_clamp_fusion), kind=kCustom, calls=%fused_computation | custom fusion | bytes 13107200 | tf_op jit(solution)/shard_map/gather | solution.py:49
  451.1 40.4 %copy.167 = f32[128,1024,12]{1,0,2:T(8,128)} copy(f32[128,1024,12]{2,1,0:T(8,128)} %bitcast.5) | data formatting | bytes 12582912 | tf_op jit(solution)/shard_map/gather | solution.py:49
  494.3 4.5 fusion.164
  503.9 4.8 fusion.120
  518.3 5.2 all-to-all-start.2
  525.2 21.8 all-gather.13.cloned.1.call-done
  548.8 25.7 %all-gather.15.cloned.1.call-done = bf16[1024,768]{1,0:T(8,128)(2,1)} async-done(((bf16[128,768]{1,0:T(8,128)(2,1)}), bf16[1024,768]{1,0:T(8,128)(2,1)}) %all-gather.15.cloned.1.call-update) | async-done | bytes 1572880 | tf_op jit(solution)/shard_map/all_gather | solution.py:106
  576.2 4.6 fusion.165
  587.6 3.5 all-to-all-start
  592.2 9.7 all-to-all-done
  601.9 5.3 fusion.166
  607.3 8.1 fusion.8
  616.5 3.2 fusion.33
  620.2 15.0 all_to_all.60
  642.4 433.3 %gather_fusion.1 = f32[131072,12]{1,0:T(8,128)} fusion(f32[12,1151]{0,1:T(8,128)S(1)} %copy.144, s32[131072]{0:T(1024)S(1)} %fusion.141), kind=kCustom, calls=%fused_computation.1 | custom fusion | bytes 13107200 | tf_op jit(solution)/shard_map/gather | solution.py:49
  1075.7 37.0 %copy.168 = f32[1024,128,12]{1,0,2:T(8,128)} copy(f32[1024,128,12]{2,1,0:T(8,128)} %bitcast.51) | data formatting | bytes 12582912 | tf_op jit(solution)/shard_map/gather | solution.py:49
  1116.1 9.1 all_gather.49
  1126.9 9.0 all_gather.45
  1135.9 7.3 fusion.3
  1146.0 9.2 all_gather.47
  1155.3 5.1 subtract_multiply_fusion.1
  1165.3 2.6 copy.146
  1167.9 4.5 fusion.100
  1172.4 6.9 fusion.110
  1181.5 2.9 multiply_reduce_fusion.1
  1185.5 4.2 fusion.9
  1194.1 7.3 fusion.1
  1207.7 2.5 pad_maximum_fusion.3
  1210.2 8.3 copy.156
  1219.6 4.6 subtract_multiply_fusion
  1228.6 2.5 pad_maximum_fusion
  1231.1 8.2 copy.153
  1239.3 9.9 all_gather.51
  1254.8 3.6 fusion.106
  1260.1 2.5 pad_maximum_fusion.2
  1262.6 8.2 copy.155
  1270.8 6.4 fusion.109
  1281.5 8.2 copy.154
  1291.3 5.6 convolution_convert_fusion.1
  1298.9 6.2 convolution_convert_fusion
  1305.1 6.2 fusion.162
  1312.3 6.5 fusion.152
  1318.8 5.6 fusion.32
  1325.6 3.5 all-to-all-start.1
  1329.0 48.6 %rev.7 = f32[12,128,1024]{2,1,0:T(8,128)} reverse(f32[12,128,1024]{2,1,0:T(8,128)} %copy-done.4), dimensions={1} | reverse | bytes 12582912 | tf_op jit(solution)/shard_map/rev | solution.py:55
  1377.6 3.8 pad.8
  1382.2 5.5 copy.173
  1387.7 3.9 slice.73
  1391.5 17.1 reshape.339
  1408.7 4.5 reduce_sum.189
  1414.3 48.5 %rev.6 = f32[12,128,1024]{2,1,0:T(8,128)} reverse(f32[12,128,1024]{2,1,0:T(8,128)} %copy-done.5), dimensions={1} | reverse | bytes 12582912 | tf_op jit(solution)/shard_map/rev | solution.py:55
  1462.8 3.5 pad.7
  1467.1 5.5 copy.172
  1472.6 3.9 slice.72
  1476.5 15.9 reshape.337
  1492.4 3.6 reduce_sum.188
  1502.1 42.1 %all-reduce.8 = (f32[4,768]{1,0:T(4,128)S(1)}, f32[384]{0:T(512)S(1)}) all-reduce(f32[4,768]{1,0:T(4,128)S(1)} %pad_maximum_fusion.4, f32[384]{0:T(512)S(1)} %reshape.340), channel_id=6, replica_groups=mesh['dp'=4,'ctx'=2,'exp'=4] {'dp','ctx','exp'}, use_global_device_ids=true, to_apply=%region_24.25.clone | all-reduce | flops 3456 | bytes 27648
  1546.3 50.2 %all-reduce.12.cloned.1.call-done = (f32[2,768,768]{1,0,2:T(2,128)}, f32[2,768,768]{1,0,2:T(2,128)}, f32[2,768,768]{1,0,2:T(2,128)}, f32[2,768,768]{1,0,2:T(2,128)}) async-done(((f32[2,768,768]{1,0,2:T(2,128)}, f32[2,768,768]{1,0,2:T(2,128)}, f32[2,768,768]{1,0,2:T(2,128)}, f32[2,768,768]{1,0,2:T(2,128)}), (f32[2,768,768]{1,0,2:T(2,128)}, f32[2,768,768]{1,0,2:T(2,128)}, f32[2,768,768]{1,0,2:T(2,128)}, ...) | async-done | bytes 18874384
  1601.2 158.8 %reduce-scatter.10.cloned.1.call-done = bf16[2,768,768]{2,1,0:T(8,128)(2,1)} async-done(((bf16[2,768,3072]{2,1,0:T(8,128)(2,1)}), bf16[2,768,768]{2,1,0:T(8,128)(2,1)}) %reduce-scatter.10.cloned.1.call-update) | async-done | bytes 2359312 | tf_op jit(solution)/shard_map/reduce_scatter | solution.py:365
  1760.0 4.2 convert_element_type.270
  1764.2 160.3 %reduce-scatter.12.cloned.1.call-done = bf16[2,768,768]{2,1,0:T(8,128)(2,1)} async-done(((bf16[2,3072,768]{2,1,0:T(8,128)(2,1)}), bf16[2,768,768]{2,1,0:T(8,128)(2,1)}) %reduce-scatter.12.cloned.1.call-update) | async-done | bytes 2359312 | tf_op jit(solution)/shard_map/reduce_scatter | solution.py:368
  1924.5 4.2 convert_element_type.272
  1928.7 138.5 %reduce-scatter.6.cloned.1.call-done = f32[768,96]{0,1:T(8,128)} async-done(((f32[768,3072]{0,1:T(8,128)}), f32[768,96]{0,1:T(8,128)}) %reduce-scatter.6.cloned.1.call-update) | async-done | bytes 294928 | tf_op jit(solution)/shard_map/reduce_scatter | solution.py:361
  2067.2 142.1 %reduce-scatter.8.cloned.1.call-done = f32[96,768]{1,0:T(8,128)} async-done(((f32[3072,768]{1,0:T(8,128)}), f32[96,768]{1,0:T(8,128)}) %reduce-scatter.8.cloned.1.call-update) | async-done | bytes 294928 | tf_op jit(solution)/shard_map/reduce_scatter | solution.py:362
  (384 shorter events, 113.8 us)
Async XLA Ops:
  7.2 9.4 copy-start
  7.2 485.4 %all-gather.9.cloned.1.call-start = ((), (), s32[]{:S(2)}) async-start(), calls=%async_computation.8 | async-start | bytes 1769472 | tf_op jit(solution)/shard_map/all_gather | solution.py:105
  8.7 7.8 copy-start.79
  10.4 6.1 copy-start.96
  11.5 480.1 %copy-start.47 = (bf16[128,768]{1,0:T(8,128)(2,1)}, bf16[128,768]{1,0:T(8,128)(2,1)S(1)}, u32[]{:S(2)}) copy-start(bf16[128,768]{1,0:T(8,128)(2,1)S(1)} %multiply_convert_fusion.14) | copy-start | bytes 589828
  13.9 488.2 %all-gather.11.cloned.1.call-start = ((), (), s32[]{:S(2)}) async-start(), calls=%async_computation.9 | async-start | bytes 1769472 | tf_op jit(solution)/shard_map/all_gather | solution.py:106
  16.3 530.7 %all-gather.13.cloned.1.call-start = ((), (), s32[]{:S(2)}) async-start(), calls=%async_computation.10 | async-start | bytes 1769472 | tf_op jit(solution)/shard_map/all_gather | solution.py:105
  451.1 40.4 %copy-start.53 = (bf16[2,768,768]{2,1,0:T(8,128)(2,1)S(1)}, bf16[2,768,768]{2,1,0:T(8,128)(2,1)}, u32[]{:S(2)}) copy-start(bf16[2,768,768]{2,1,0:T(8,128)(2,1)} %param.16) | copy-start | bytes 7077892
  503.8 5.9 slice-start.3
  503.8 5.9 slice-start.4
  503.8 6.8 slice-start.7
  512.8 11.3 copy-start.54
  513.3 11.1 copy-start.50
  514.4 60.1 %all-gather.15.cloned.1.call-start = ((), (), s32[]{:S(2)}) async-start(), calls=%async_computation.11 | async-start | bytes 1769472 | tf_op jit(solution)/shard_map/all_gather | solution.py:106
  517.2 31.5 %copy-start.90 = (s32[128]{0:T(128)}, s32[128]{0:T(128)S(1)}, u32[]{:S(2)}) copy-start(s32[128]{0:T(128)S(1)} %multiply_add_fusion) | copy-start | bytes 1540
  518.3 69.2 %all-to-all-start.2 = ((bf16[8,2,16,768]{3,2,1,0:T(8,128)(2,1)}), bf16[8,2,16,768]{3,2,1,0:T(8,128)(2,1)}, u32[]{:S(2)}, u32[]{:S(2)}) async-start(bf16[8,2,16,768]{3,2,1,0:T(8,128)(2,1)} %bitcast.35), calls=%async_computation.2 | async-start | bytes 786432 | tf_op jit(solution)/shard_map/all_to_all | solution.py:262
  523.5 590.8 %all-gather.21.cloned.1.call-start = ((), (), s32[]{:S(2)}) async-start(), calls=%async_computation.14 | async-start | bytes 1769472 | tf_op jit(solution)/shard_map/all_gather | solution.py:196
  524.4 24.3 %copy-start.74 = (bf16[128,768]{1,0:T(8,128)(2,1)}, bf16[128,768]{1,0:T(8,128)(2,1)S(1)}, u32[]{:S(2)}) copy-start(bf16[128,768]{1,0:T(8,128)(2,1)S(1)} %fusion.85) | copy-start | bytes 589828
  548.7 32.1 %copy-start.8 = (bf16[1024,768]{0,1:T(8,128)(2,1)}, bf16[1024,768]{0,1:T(8,128)(2,1)S(1)}, u32[]{:S(2)}) copy-start(bf16[1024,768]{0,1:T(8,128)(2,1)S(1)} %copy.131) | copy-start | bytes 4718596
  576.2 7.3 copy-start.12
  585.1 22.1 copy-start.45
  585.8 50.4 %copy-start.17 = (f32[128,768]{1,0:T(8,128)}, f32[128,768]{1,0:T(8,128)S(1)}, u32[]{:S(2)}) copy-start(f32[128,768]{1,0:T(8,128)S(1)} %get-tuple-element.101) | copy-start | bytes 1179652
  586.5 20.8 copy-start.94
  587.6 14.3 all-to-all-start
  591.0 534.1 %all-gather.17.cloned.1.call-start = ((), (), s32[]{:S(2)}) async-start(), calls=%async_computation.12 | async-start | bytes 1769472 | tf_op jit(solution)/shard_map/all_gather | solution.py:196
  592.1 15.2 copy-start.75
  592.1 573.2 %all-gather.19.cloned.1.call-start = ((), (), s32[]{:S(2)}) async-start(), calls=%async_computation.13 | async-start | bytes 1769472 | tf_op jit(solution)/shard_map/all_gather | solution.py:197
  601.9 14.6 slice-start
  601.9 14.6 slice-start.1
  607.2 8.1 copy-start.13
  607.3 9.3 slice-start.2
  619.8 15.5 copy-start.82
  619.8 15.5 copy-start.92
  619.8 15.5 copy-start.95
  619.8 16.4 copy-start.69
  619.8 16.4 copy-start.106
  619.8 16.6 copy-start.23
  636.4 439.3 %copy-start.36 = (f32[128,768]{1,0:T(8,128)}, f32[128,768]{1,0:T(8,128)S(1)}, u32[]{:S(2)}) copy-start(f32[128,768]{1,0:T(8,128)S(1)} %subtract_add_fusion.3) | copy-start | bytes 1179652
  637.7 615.4 %all-gather.23.cloned.1.call-start = ((), (), s32[]{:S(2)}) async-start(), calls=%async_computation.15 | async-start | bytes 1769472 | tf_op jit(solution)/shard_map/all_gather | solution.py:197
  1075.7 37.0 %copy-start.72 = (bf16[128,768]{1,0:T(8,128)(2,1)S(1)}, bf16[128,768]{1,0:T(8,128)(2,1)}, u32[]{:S(2)}) copy-start(bf16[128,768]{1,0:T(8,128)(2,1)} %fusion.88) | copy-start | bytes 589828
  1075.7 37.8 %copy-start.73 = (bf16[128,768]{1,0:T(8,128)(2,1)S(1)}, bf16[128,768]{1,0:T(8,128)(2,1)}, u32[]{:S(2)}) copy-start(bf16[128,768]{1,0:T(8,128)(2,1)} %fusion.91) | copy-start | bytes 589828
  1172.4 9.1 copy-start.99
  1179.3 6.1 copy-start.20
  1179.3 10.4 slice-start.5
  1185.5 6.6 copy-start.40
  1192.3 13.7 copy-start.34
  1193.6 402.9 %all-reduce.12.cloned.1.call-start = ((), (), s32[]{:S(2)}) async-start(), calls=%async_computation.20 | async-start | bytes 37748736
  1194.0 7.4 copy-start.51
  1194.0 7.3 copy-start.67
  1194.1 9.3 copy-start.37
  1194.1 9.3 copy-start.46
  1210.2 9.4 copy-start.11
  1231.1 18.1 copy-start.52
  1231.1 18.1 copy-start.65
  1231.1 20.0 copy-start.64
  1289.7 470.3 %reduce-scatter.10.cloned.1.call-start = ((), (), s32[]{:S(2)}) async-start(), calls=%async_computation.18 | async-start | bytes 11796480 | tf_op jit(solution)/shard_map/reduce_scatter | solution.py:365
  1296.9 627.6 %reduce-scatter.12.cloned.1.call-start = ((), (), s32[]{:S(2)}) async-start(), calls=%async_computation.19 | async-start | bytes 11796480 | tf_op jit(solution)/shard_map/reduce_scatter | solution.py:368
  1305.1 762.1 %reduce-scatter.6.cloned.1.call-start = ((), (), s32[]{:S(2)}) async-start(), calls=%async_computation.16 | async-start | bytes 9732096 | tf_op jit(solution)/shard_map/reduce_scatter | solution.py:361
  1311.3 898.0 %reduce-scatter.8.cloned.1.call-start = ((), (), s32[]{:S(2)}) async-start(), calls=%async_computation.17 | async-start | bytes 9732096 | tf_op jit(solution)/shard_map/reduce_scatter | solution.py:362
  1325.6 87.6 %all-to-all-start.1 = ((bf16[1,2,128,768]{3,1,0,2:T(2,128)(2,1)}), bf16[1,2,128,768]{3,1,0,2:T(2,128)(2,1)S(1)}, u32[]{:S(2)}, u32[]{:S(2)}) async-start(bf16[1,2,128,768]{3,1,0,2:T(2,128)(2,1)} %copy.134), calls=%async_computation.1 | async-start | bytes 786432 | tf_op jit(solution)/shard_map/all_to_all | solution.py:311
  1498.0 47.4 %copy-start.35 = (f32[128,768]{1,0:T(8,128)S(1)}, f32[128,768]{1,0:T(8,128)}, u32[]{:S(2)}) copy-start(f32[128,768]{1,0:T(8,128)} %copy-done.34) | copy-start | bytes 1179652
  1498.5 46.9 %copy-start.97 = (f32[128]{0:T(128)S(1)}, f32[128]{0:T(128)}, u32[]{:S(2)}) copy-start(f32[128]{0:T(128)} %copy-done.96) | copy-start | bytes 1540
  1498.5 46.9 %copy-start.103 = (f32[128]{0:T(128)S(1)}, f32[128]{0:T(128)}, u32[]{:S(2)}) copy-start(f32[128]{0:T(128)} %get-tuple-element.84) | copy-start | bytes 1540
  1760.0 449.3 %copy-start.1 = (f32[32,12]{0,1:T(8,128)S(1)}, f32[32,12]{0,1:T(8,128)}, u32[]{:S(2)}) copy-start(f32[32,12]{0,1:T(8,128)} %param.21) | copy-start | bytes 4612
  (68 other events, 226.6 us)
Sparse Core Ops, SparseCore 0:
  14.0 28.3 all-gather.8
  44.9 25.6 all-gather.10
  514.5 32.4 all-gather.12
  548.7 25.6 all-gather.14
  576.2 27.9 all-gather.20
  605.9 29.8 all-gather.16
  637.8 25.6 all-gather.18
  1193.7 25.6 all-gather.22
  1289.9 306.5 all-reduce.11
  1598.7 161.3 reduce-scatter.9
  1762.4 162.1 reduce-scatter.11
  1930.9 136.3 reduce-scatter.5
  2074.7 134.6 reduce-scatter.7
where the time goes:
time: 2230 us; the launch traced here: 2220 us
  local copies, waits for them, and re-layouts  1190 us (53%)
  waiting for transfers between devices  707 us (32%)
  matrix products  156 us (7%)
  blocking collectives  94.3 us (4%)
  other arithmetic  41 us (2%)
    gather x4, local copies, waits for them, and re-layouts, bias_block(): return window[:, offsets]  944 us
    reduce_scatter x1, waiting for transfers between devices, body(): lax.psum_scatter(grad_eout.astype(jnp.bfloat16), 'dp', scatter_dimension=...  160 us
    reduce_scatter x1, waiting for transfers between devices, body(): lax.psum_scatter(grad_ein.astype(jnp.bfloat16), 'dp', scatter_dimension=2...  159 us
    reduce_scatter x1, waiting for transfers between devices, body(): lax.psum_scatter(grad_dout, ('dp', 'ctx', 'exp'), scatter_dimension=0, ti...  142 us
    reduce_scatter x1, waiting for transfers between devices, body(): lax.psum_scatter(grad_din, ('dp', 'ctx', 'exp'), scatter_dimension=1, til...  138 us
    rev x2, local copies, waits for them, and re-layouts, add_diagonals(): flipped = d_scores[:, ::-1, :]  97 us
    unnamed x14, waiting for transfers between devices  50.4 us
  transfers between devices with their start and end apart: 16, of which 8 were waited for; matrix products, arithmetic and copies ran while one was open for 58% of the time, Pallas kernels for 0%

commit v1 on v0

v1 whole, which is shorter than its diff:
```python
import functools

import jax
import jax.numpy as jnp
from jax import lax
from jax.experimental import pallas as pl
from jax.experimental.pallas import tpu as pltpu
from jax.sharding import PartitionSpec as P

epsilon = 1e-06
highest = lax.Precision.HIGHEST
MESH = pl.DeviceIdType.MESH
VMEM = pltpu.VMEM


def to_half(values):
    return values.astype(jnp.bfloat16)


def widen(values):
    return values.astype(jnp.float32)


def dot_nn(a, b):
    return jnp.dot(a, b, preferred_element_type=jnp.float32)


def dot_nt(a, b):
    return lax.dot_general(a, b, (((1,), (1,)), ((), ())), preferred_element_type=jnp.float32)


def dot_tn(a, b):
    return lax.dot_general(a, b, (((0,), (0,)), ((), ())), preferred_element_type=jnp.float32)


def rotate(values, shift):
    width = values.shape[-1]
    shift = shift % width
    return values if shift == 0 else pltpu.roll(values, shift, values.ndim - 1)


def pad_lanes(values, width):
    if values.shape[1] == width:
        return values
    zeros = jnp.zeros((values.shape[0], width - values.shape[1]), values.dtype)
    return jnp.concatenate([values, zeros], axis=1)


class Plan:
    def __init__(self, cycle, exp_size, head_count, head_size, rows):
        self.cycle, self.exp_size, self.rows = cycle, exp_size, rows
        groups = 1
        while cycle % (groups * 2) == 0 and head_count % (groups * 2) == 0:
            groups *= 2
        self.groups, self.splits = groups, cycle // groups
        self.heads, self.head_size = head_count // groups, head_size
        self.width = self.heads * head_size
        self.model = head_count * head_size
        self.length = cycle * rows
        self.wide = -(-self.width // 128) * 128
        self.lead = self.wide - self.width
        self.pair = 2 * self.width
        self.tiled = self.heads if self.heads * rows * self.length * 8 <= 4 << 20 else 1
        assert self.pair % 128 == 0 and self.pair - self.wide == self.width - self.lead

    def place(self):
        c = lax.axis_index("ctx") * self.exp_size + lax.axis_index("exp")
        return c, c // self.splits, lax.rem(c, self.splits)

    def device(self, c):
        return (lax.axis_index("dp"), c // self.exp_size, lax.rem(c, self.exp_size))

    def peer(self, c, step):
        return lax.rem(c + step, self.cycle)


def greet(plan, c):
    barrier = pltpu.get_barrier_semaphore()
    for step in range(1, plan.cycle):
        pl.semaphore_signal(
            barrier, inc=1, device_id=plan.device(plan.peer(c, step)), device_id_type=MESH
        )
    return barrier


def rms_normed(hidden, gains):
    inv_rms = lax.rsqrt(jnp.mean(hidden * hidden, axis=-1, keepdims=True) + epsilon)
    return hidden * inv_rms * gains, inv_rms


def fill_bias(plan, rows_ref, tiles, heads):
    for head in heads:
        row = jnp.broadcast_to(rows_ref[head : head + 1, :], (plan.rows, 2 * plan.length))
        tiles[head % plan.tiled] = pltpu.roll(row, 0, 1, stride=1, stride_axis=0)


def bias_part(plan, tiles, head, key_block, split):
    parts = []
    head = head % plan.tiled
    for block in range(plan.groups):
        first = plan.length + (block * plan.splits + split - key_block) * plan.rows
        parts.append(tiles[head, :, pl.ds(pl.multiple_of(first, plan.rows), plan.rows)])
    return jnp.concatenate(parts, axis=1)


def lanes_between(shape, low, high):
    lane = lax.broadcasted_iota(jnp.int32, shape, 1)
    return (lane >= low) & (lane < high)


def natural(plan, blocks, lead):
    total = None
    for group, block in enumerate(blocks):
        moved = rotate(pad_lanes(block, plan.model), group * plan.width - lead)
        total = moved if total is None else total + moved
    return total


def remote(src, dst, send, recv, device):
    return pltpu.make_async_remote_copy(
        src_ref=src, dst_ref=dst, send_sem=send, recv_sem=recv, device_id=device, device_id_type=MESH
    )


def forward_kernel(
    plan,
    layer,
    x_ref,
    gain_ref,
    bias_ref,
    wq_hbm,
    wk_hbm,
    wv_hbm,
    wo_hbm,
    mid_ref,
    normed_ref,
    query_ref,
    pair_ref,
    heads_ref,
    attended_ref,
    norm_ref,
    weights,
    tiles,
    send_pair,
    send_query,
    scores,
    probs,
    att_in,
    load_sem,
    pair_send,
    pair_recv,
    query_send,
    query_recv,
    att_send,
    att_recv,
):
    c, group, split = plan.place()
    loads = []
    for slot, source in enumerate((wv_hbm, wk_hbm, wq_hbm, wo_hbm)):
        load = pltpu.make_async_copy(source.at[layer], weights.at[slot], load_sem.at[slot])
        load.start()
        loads.append(load)
    barrier = greet(plan, c)
    hidden = x_ref[...]
    normed, _ = rms_normed(hidden, gain_ref[layer * 2 : layer * 2 + 1, :])
    normed_half = to_half(normed)
    normed_ref[...] = normed_half
    loads[0].wait()
    values = dot_nn(normed_half, weights[0])
    loads[1].wait()
    keys = dot_nn(normed_half, weights[1])
    is_value = lanes_between((plan.rows, plan.pair), 0, plan.width)
    for g in range(plan.groups):
        value_part = rotate(values, -g * plan.width)[:, : plan.pair]
        key_part = rotate(keys, (1 - g) * plan.width)[:, : plan.pair]
        send_pair[g] = to_half(jnp.where(is_value, value_part, key_part))
    pl.semaphore_wait(barrier, plan.cycle - 1)
    copies = []
    for step in range(1, plan.cycle):
        to = plan.peer(c, step)
        copy = remote(
            send_pair.at[to // plan.splits],
            pair_ref.at[c],
            pair_send.at[step],
            pair_recv.at[step],
            plan.device(to),
        )
        copy.start()
        copies.append(copy)
    loads[2].wait()
    queries = dot_nn(normed_half, weights[2])
    is_query = lanes_between((plan.rows, plan.wide), plan.lead, plan.wide)
    for g in range(plan.groups):
        query_part = rotate(queries, plan.lead - g * plan.width)[:, : plan.wide]
        send_query[g] = to_half(jnp.where(is_query, query_part, 0.0))
    for step in range(1, plan.groups):
        to = plan.peer(c, step * plan.splits)
        copy = remote(
            send_query.at[to // plan.splits],
            query_ref.at[group],
            query_send.at[step],
            query_recv.at[step],
            plan.device(to),
        )
        copy.start()
        copies.append(copy)
    pair_ref[c] = send_pair[group]
    query_ref[group] = send_query[group]
    fill_bias(plan, bias_ref, tiles, range(plan.tiled))
    for copy in copies:
        copy.wait()

    total = plan.groups * plan.rows
    queries_all = query_ref[...].reshape(total, plan.wide)
    values_t = jnp.transpose(pair_ref[...].reshape(plan.length, plan.pair)[:, : plan.wide])
    rows_t = []
    for head in range(plan.heads):
        if head >= plan.tiled:
            fill_bias(plan, bias_ref, tiles, [head])
        low = plan.lead + head * plan.head_size
        picked = jnp.where(
            lanes_between(queries_all.shape, low, low + plan.head_size), queries_all, 0
        )

        def score_block(block, top):
            part = dot_nt(pair_ref[block][:, plan.pair - plan.wide :], picked)
            part = part + bias_part(plan, tiles, head, block, split)
            scores[pl.ds(pl.multiple_of(block * plan.rows, plan.rows), plan.rows), :] = part
            return jnp.maximum(top, jnp.max(part, axis=0, keepdims=True))

        top = lax.fori_loop(0, plan.cycle, score_block, jnp.full((1, total), -1e30, jnp.float32))

        def weight_block(block, norm):
            where = pl.ds(pl.multiple_of(block * plan.rows, plan.rows), plan.rows)
            part = jnp.exp(scores[where, :] - top)
            probs[where, :] = to_half(part)
            return norm + jnp.sum(part, axis=0, keepdims=True)

        norm = lax.fori_loop(0, plan.cycle, weight_block, jnp.zeros((1, total), jnp.float32))
        norm_ref[head : head + 1, :] = top + jnp.log(norm)
        mine = values_t[head * plan.head_size : (head + 1) * plan.head_size, :]
        rows_t.append(dot_nn(mine, probs[...]) / norm)
    rows_t.append(jnp.zeros((plan.lead, total), jnp.float32))
    heads_ref[...] = to_half(jnp.transpose(jnp.concatenate(rows_t, axis=0))).reshape(
        plan.groups, plan.rows, plan.wide
    )
    copies = []
    for step in range(1, plan.groups):
        to = plan.peer(c, step * plan.splits)
        copy = remote(
            heads_ref.at[to // plan.splits],
            att_in.at[group],
            att_send.at[step],
            att_recv.at[step],
            plan.device(to),
        )
        copy.start()
        copies.append(copy)
    att_in[group] = heads_ref[group]
    loads[3].wait()
    for copy in copies:
        copy.wait()
    attended = to_half(natural(plan, [widen(att_in[g]) for g in range(plan.groups)], 0))
    attended_ref[...] = attended
    mid_ref[...] = hidden + dot_nn(attended, weights[3])


def attention_forward(plan, layer, hidden, gains, bias_rows, wq, wk, wv, wo, collective):
    f32, half = jnp.float32, jnp.bfloat16
    total = plan.groups * plan.rows
    whole = pl.BlockSpec(memory_space=VMEM)
    hbm = pl.BlockSpec(memory_space=pl.ANY)
    dma = pltpu.SemaphoreType.DMA
    return pl.pallas_call(
        functools.partial(forward_kernel, plan, layer),
        out_shape=(
            jax.ShapeDtypeStruct((plan.rows, plan.model), f32),
            jax.ShapeDtypeStruct((plan.rows, plan.model), half),
            jax.ShapeDtypeStruct((plan.groups, plan.rows, plan.wide), half),
            jax.ShapeDtypeStruct((plan.cycle, plan.rows, plan.pair), half),
            jax.ShapeDtypeStruct((plan.groups, plan.rows, plan.wide), half),
            jax.ShapeDtypeStruct((plan.rows, plan.model), half),
            jax.ShapeDtypeStruct((plan.heads, total), f32),
        ),
        in_specs=[whole, whole, whole, hbm, hbm, hbm, hbm],
        out_specs=(whole,) * 7,
        scratch_shapes=[
            VMEM((4, plan.model, plan.model), half),
            VMEM((plan.tiled, plan.rows, 2 * plan.length), f32),
            VMEM((plan.groups, plan.rows, plan.pair), half),
            VMEM((plan.groups, plan.rows, plan.wide), half),
            VMEM((plan.length, total), f32),
            VMEM((plan.length, total), half),
            VMEM((plan.groups, plan.rows, plan.wide), half),
            dma((4,)),
            dma((plan.cycle,)),
            dma((plan.cycle,)),
            dma((plan.groups,)),
            dma((plan.groups,)),
            dma((plan.groups,)),
            dma((plan.groups,)),
        ],
        compiler_params=pltpu.CompilerParams(
            collective_id=collective, has_side_effects=True, vmem_limit_bytes=56 * 1024 * 1024
        ),
        name="attention_forward",
    )(hidden, gains, bias_rows, wq, wk, wv, wo)


def backward_kernel(
    plan,
    layer,
    grad_ref,
    x_ref,
    gain_ref,
    bias_ref,
    normed_ref,
    query_ref,
    pair_ref,
    heads_ref,
    attended_ref,
    norm_ref,
    wq_hbm,
    wk_hbm,
    wv_hbm,
    wo_hbm,
    out_ref,
    gain_grad_ref,
    weight_grad_ref,
    bias_grad_ref,
    weights,
    tiles,
    sums,
    send_grad,
    grad_in,
    probs,
    slopes,
    key_sum,
    value_sum,
    send_pair,
    pair_in,
    send_query,
    query_in,
    load_sem,
    grad_send,
    grad_recv,
    pair_send,
    pair_recv,
    query_send,
    query_recv,
):
    c, group, split = plan.place()
    total = plan.groups * plan.rows
    loads = []
    for slot, source in enumerate((wv_hbm, wk_hbm, wq_hbm, wo_hbm)):
        load = pltpu.make_async_copy(source.at[layer], weights.at[slot], load_sem.at[slot])
        loads.append(load)
    for slot in (3, 0, 1, 2):
        loads[slot].start()
    barrier = greet(plan, c)
    grad = grad_ref[...]
    grad_half = to_half(grad)
    loads[3].wait()
    d_attended = dot_nt(grad_half, weights[3])
    in_group = lanes_between((plan.rows, plan.wide), 0, plan.width)
    for g in range(plan.groups):
        part = rotate(d_attended, -g * plan.width)[:, : plan.wide]
        send_grad[g] = to_half(jnp.where(in_group, part, 0.0))
    pl.semaphore_wait(barrier, plan.cycle - 1)
    copies = []
    for step in range(1, plan.groups):
        to = plan.peer(c, step * plan.splits)
        copy = remote(
            send_grad.at[to // plan.splits],
            grad_in.at[group],
            grad_send.at[step],
            grad_recv.at[step],
            plan.device(to),
        )
        copy.start()
        copies.append(copy)
    grad_in[group] = send_grad[group]
    fill_bias(plan, bias_ref, tiles, range(plan.tiled))
    weight_grad_ref[3] = to_half(dot_tn(attended_ref[...], grad_half))
    queries_all = query_ref[...].reshape(total, plan.wide)
    keys_t = jnp.transpose(
        pair_ref[...].reshape(plan.length, plan.pair)[:, plan.pair - plan.wide :]
    )
    heads_t = jnp.transpose(widen(heads_ref[...].reshape(total, plan.wide)))
    for copy in copies:
        copy.wait()
    grads_all = grad_in[...].reshape(total, plan.wide)
    grads_t = jnp.transpose(widen(grads_all))
    products_t = grads_t * heads_t
    query_rows_t = [jnp.zeros((plan.lead, total), jnp.float32)]
    for head in range(plan.heads):
        if head >= plan.tiled:
            fill_bias(plan, bias_ref, tiles, [head])
        low, high = head * plan.head_size, (head + 1) * plan.head_size
        picked_queries = jnp.where(
            lanes_between(queries_all.shape, plan.lead + low, plan.lead + high), queries_all, 0
        )
        picked_grads = jnp.where(lanes_between(grads_all.shape, low, high), grads_all, 0)
        delta = jnp.sum(products_t[low:high, :], axis=0, keepdims=True)
        log_norm = norm_ref[head : head + 1, :]
        sums[...] = jnp.zeros_like(sums)

        def slope_block(block, carry):
            where = pl.ds(pl.multiple_of(block * plan.rows, plan.rows), plan.rows)
            part = dot_nt(pair_ref[block][:, plan.pair - plan.wide :], picked_queries)
            part = part + bias_part(plan, tiles, head, block, split)
            part = jnp.exp(part - log_norm)
            probs[where, :] = to_half(part)
            slope = part * (dot_nt(pair_ref[block][:, : plan.wide], picked_grads) - delta)
            slopes[where, :] = to_half(slope)
            for b in range(plan.groups):
                first = plan.length + (b * plan.splits + split - block) * plan.rows
                at = pl.ds(pl.multiple_of(first, plan.rows), plan.rows)
                sums[:, at] += slope[:, b * plan.rows : (b + 1) * plan.rows]
            return carry

        lax.fori_loop(0, plan.cycle, slope_block, 0)
        key_part = dot_nn(slopes[...], picked_queries)
        value_part = dot_nn(probs[...], picked_grads)
        if head == 0:
            key_sum[...], value_sum[...] = key_part, value_part
        else:
            key_sum[...] += key_part
            value_sum[...] += value_part
        query_rows_t.append(dot_nn(keys_t[plan.lead + low : plan.lead + high, :], slopes[...]))
        row = lax.broadcasted_iota(jnp.int32, (plan.rows, plan.rows), 0)
        column = lax.broadcasted_iota(jnp.int32, (plan.rows, plan.rows), 1)
        flip = (row + column == plan.rows - 1).astype(jnp.float32)
        flipped = jnp.dot(flip, sums[...], precision=highest, preferred_element_type=jnp.float32)
        skewed = pltpu.roll(
            flipped, 2 * plan.length - (plan.rows - 1), 1, stride=1, stride_axis=0
        )
        bias_grad_ref[head : head + 1, :] = jnp.sum(skewed, axis=0, keepdims=True)
    send_query[...] = to_half(jnp.transpose(jnp.concatenate(query_rows_t, axis=0))).reshape(
        plan.groups, plan.rows, plan.wide
    )
    value_all, key_all = value_sum[...], key_sum[...]
    low, gap = plan.pair - plan.wide, plan.wide - (plan.pair - plan.wide)
    middle = jnp.where(
        lanes_between((plan.length, gap), 0, plan.width - low), value_all[:, low:], key_all[:, :gap]
    )
    send_pair[...] = to_half(
        jnp.concatenate([value_all[:, :low], middle, key_all[:, gap:]], axis=1)
    ).reshape(plan.cycle, plan.rows, plan.pair)
    copies = []
    for step in range(1, plan.cycle):
        to = plan.peer(c, step)
        copy = remote(
            send_pair.at[to], pair_in.at[c], pair_send.at[step], pair_recv.at[step], plan.device(to)
        )
        copy.start()
        copies.append(copy)
    for step in range(1, plan.groups):
        to = plan.peer(c, step * plan.splits)
        copy = remote(
            send_query.at[to // plan.splits],
            query_in.at[group],
            query_send.at[step],
            query_recv.at[step],
            plan.device(to),
        )
        copy.start()
        copies.append(copy)
    pair_in[c] = send_pair[c]
    query_in[group] = send_query[group]
    hidden = x_ref[...]
    gains = gain_ref[layer * 2 : layer * 2 + 1, :]
    inv_rms = lax.rsqrt(jnp.mean(hidden * hidden, axis=-1, keepdims=True) + epsilon)
    for slot in range(3):
        loads[slot].wait()
    for copy in copies:
        copy.wait()
    is_value = lanes_between((plan.rows, plan.pair), 0, plan.width)
    value_blocks, key_blocks = [], []
    for g in range(plan.groups):
        block = widen(pair_in[g * plan.splits])
        for other in range(1, plan.splits):
            block = block + widen(pair_in[g * plan.splits + other])
        value_blocks.append(jnp.where(is_value, block, 0.0))
        key_blocks.append(jnp.where(is_value, 0.0, block))
    d_values = to_half(natural(plan, value_blocks, 0))
    d_keys = to_half(natural(plan, key_blocks, plan.width))
    d_queries = to_half(
        natural(plan, [widen(query_in[g]) for g in range(plan.groups)], plan.lead)
    )
    normed_half = normed_ref[...]
    d_normed = (
        dot_nt(d_queries, weights[2]) + dot_nt(d_keys, weights[1]) + dot_nt(d_values, weights[0])
    )
    weight_grad_ref[0] = to_half(dot_tn(normed_half, d_queries))
    weight_grad_ref[1] = to_half(dot_tn(normed_half, d_keys))
    weight_grad_ref[2] = to_half(dot_tn(normed_half, d_values))
    d_scaled = d_normed * gains
    gain_grad_ref[...] = jnp.sum(d_normed * hidden * inv_rms, axis=0, keepdims=True)
    out_ref[...] = (
        grad
        + inv_rms * d_scaled
        - hidden * (inv_rms * inv_rms * inv_rms) * jnp.mean(d_scaled * hidden, axis=-1, keepdims=True)
    )


def attention_backward(plan, layer, grad, cache, gains, bias_rows, wq, wk, wv, wo, collective):
    f32, half = jnp.float32, jnp.bfloat16
    total = plan.groups * plan.rows
    whole = pl.BlockSpec(memory_space=VMEM)
    hbm = pl.BlockSpec(memory_space=pl.ANY)
    dma = pltpu.SemaphoreType.DMA
    hidden, normed, query, pair, heads, attended, norm = cache
    block = (plan.groups, plan.rows, plan.wide)
    pairs = (plan.cycle, plan.rows, plan.pair)
    return pl.pallas_call(
        functools.partial(backward_kernel, plan, layer),
        out_shape=(
            jax.ShapeDtypeStruct((plan.rows, plan.model), f32),
            jax.ShapeDtypeStruct((1, plan.model), f32),
            jax.ShapeDtypeStruct((4, plan.model, plan.model), half),
            jax.ShapeDtypeStruct((plan.heads, 2 * plan.length), f32),
        ),
        in_specs=[whole] * 10 + [hbm] * 4,
        out_specs=(whole,) * 4,
        scratch_shapes=[
            VMEM((4, plan.model, plan.model), half),
            VMEM((plan.tiled, plan.rows, 2 * plan.length), f32),
            VMEM((plan.rows, 2 * plan.length), f32),
            VMEM(block, half),
            VMEM(block, half),
            VMEM((plan.length, total), half),
            VMEM((plan.length, total), half),
            VMEM((plan.length, plan.wide), f32),
            VMEM((plan.length, plan.wide), f32),
            VMEM(pairs, half),
            VMEM(pairs, half),
            VMEM(block, half),
            VMEM(block, half),
            dma((4,)),
            dma((plan.groups,)),
            dma((plan.groups,)),
            dma((plan.cycle,)),
            dma((plan.cycle,)),
            dma((plan.groups,)),
            dma((plan.groups,)),
        ],
        compiler_params=pltpu.CompilerParams(
            collective_id=collective, has_side_effects=True, vmem_limit_bytes=60 * 1024 * 1024
        ),
        name="attention_backward",
    )(grad, hidden, gains, bias_rows, normed, query, pair, heads, attended, norm, wq, wk, wv, wo)


def smooth_act(values):
    return values * jax.nn.sigmoid(values)


def smooth_slope(values):
    sigma = jax.nn.sigmoid(values)
    return sigma * (1.0 + values * (1.0 - sigma))


def rms_backward(hidden, inv_rms, gains, d_normed):
    d_scaled = d_normed * gains
    d_gains = jnp.sum(d_normed * hidden * inv_rms, axis=0)
    d_hidden = inv_rms * d_scaled - hidden * inv_rms**3 * jnp.mean(
        d_scaled * hidden, axis=-1, keepdims=True
    )
    return (d_hidden, d_gains)


def along_dp(values):
    count = lax.axis_size("dp")
    return [values] + [
        lax.ppermute(values, "dp", [(i, i ^ step) for i in range(count)]) for step in range(1, count)
    ]


def body(
    inputs,
    w_query,
    w_key,
    w_value,
    w_out,
    norm_gain,
    bias_table,
    dense_in,
    dense_out,
    expert_in,
    expert_out,
    routes,
    gate_scale,
    buckets,
    cotangent,
):
    group_rows, model_width = inputs.shape
    head_count = bias_table.shape[1]
    head_size = model_width // head_count
    bucket_count = bias_table.shape[0]
    cycle_size = lax.axis_size(("ctx", "exp"))
    plan = Plan(cycle_size, lax.axis_size("exp"), head_count, head_size, group_rows)
    my_group = lax.axis_index(("ctx", "exp")) // plan.splits
    reversed_buckets = jnp.roll(buckets[::-1], 1)
    bucket_picks = (
        reversed_buckets[None, :] == jnp.arange(bucket_count, dtype=jnp.int32)[:, None]
    ).astype(jnp.float32)
    my_table = lax.dynamic_slice_in_dim(bias_table.T, my_group * plan.heads, plan.heads, 0)
    bias_rows = jnp.dot(my_table, bucket_picks, precision=highest)

    local_experts = expert_in.shape[0]
    expert_total = local_experts * cycle_size
    capacity = 2 * group_rows // expert_total
    recv_rows = cycle_size * capacity
    flat_routes = routes[:, 0]
    route_hits = (
        flat_routes[:, None] == jnp.arange(expert_total, dtype=jnp.int32)[None, :]
    ).astype(jnp.int32)
    slot_order = jnp.sum((jnp.cumsum(route_hits, axis=0) - 1) * route_hits, axis=1)
    target = flat_routes * capacity + slot_order
    dispatch = (
        target[None, :] == jnp.arange(expert_total * capacity, dtype=jnp.int32)[:, None]
    ).astype(jnp.bfloat16)

    def to_owners(rows_half):
        placed = jnp.dot(dispatch, rows_half, preferred_element_type=jnp.float32)
        return lax.all_to_all(
            to_half(placed).reshape(cycle_size, local_experts, capacity, model_width),
            ("ctx", "exp"),
            split_axis=0,
            concat_axis=2,
            tiled=True,
        ).reshape(local_experts, recv_rows, model_width)

    def from_owners(produced):
        returned = lax.all_to_all(
            produced.reshape(1, local_experts, recv_rows, model_width),
            ("ctx", "exp"),
            split_axis=2,
            concat_axis=0,
            tiled=True,
        )
        return jnp.einsum(
            "sc,sd->cd",
            dispatch,
            returned.reshape(expert_total * capacity, model_width),
            preferred_element_type=jnp.float32,
        )

    grad_rows = to_owners(to_half(gate_scale * cotangent))
    grad_rows_all = jnp.concatenate(along_dp(grad_rows), axis=1)

    mid_zero, *cache_zero = attention_forward(
        plan, 0, inputs, norm_gain, bias_rows, w_query, w_key, w_value, w_out, 0
    )
    inv_rms_one = lax.rsqrt(jnp.mean(mid_zero * mid_zero, axis=-1, keepdims=True) + epsilon)
    normed_half = to_half(mid_zero * inv_rms_one * norm_gain[1])
    pre_act = jnp.dot(normed_half, dense_in, preferred_element_type=jnp.float32)
    active = to_half(smooth_act(pre_act))
    stream = mid_zero + jnp.dot(active, dense_out, preferred_element_type=jnp.float32)
    mid_one, *cache_one = attention_forward(
        plan, 1, stream, norm_gain, bias_rows, w_query, w_key, w_value, w_out, 1
    )
    inv_rms_three = lax.rsqrt(jnp.mean(mid_one * mid_one, axis=-1, keepdims=True) + epsilon)
    rows = to_owners(to_half(mid_one * inv_rms_three * norm_gain[3]))
    rows_all = jnp.concatenate(along_dp(rows), axis=1)
    expert_pre = jnp.einsum("erd,edf->erf", rows, expert_in, preferred_element_type=jnp.float32)
    expert_active = to_half(smooth_act(expert_pre))
    produced = to_half(
        jnp.einsum("erf,efd->erd", expert_active, expert_out, preferred_element_type=jnp.float32)
    )
    d_active = jnp.einsum("erd,efd->erf", grad_rows, expert_out, preferred_element_type=jnp.float32)
    d_pre = to_half(d_active * smooth_slope(expert_pre))
    d_rows = to_half(jnp.einsum("erf,edf->erd", d_pre, expert_in, preferred_element_type=jnp.float32))
    output = mid_one + gate_scale * from_owners(produced)
    d_hidden, gains_four = rms_backward(mid_one, inv_rms_three, norm_gain[3], from_owners(d_rows))
    grad_three = cotangent + d_hidden

    grad_two, gains_three, attn_two, bias_two = attention_backward(
        plan, 1, grad_three, [stream] + cache_one, norm_gain, bias_rows, w_query, w_key, w_value, w_out, 2
    )
    grad_half = to_half(grad_two)
    grad_dout = jnp.dot(active.T, grad_half, preferred_element_type=jnp.float32)
    d_active = jnp.dot(grad_half, dense_out.T, preferred_element_type=jnp.float32)
    d_pre = to_half(d_active * smooth_slope(pre_act))
    grad_din = jnp.dot(normed_half.T, d_pre, preferred_element_type=jnp.float32)
    d_normed = jnp.dot(d_pre, dense_in.T, preferred_element_type=jnp.float32)
    d_hidden, gains_two = rms_backward(mid_zero, inv_rms_one, norm_gain[1], d_normed)
    grad_one = grad_two + d_hidden
    input_grad, gains_one, attn_one, bias_one = attention_backward(
        plan, 0, grad_one, [inputs] + cache_zero, norm_gain, bias_rows, w_query, w_key, w_value, w_out, 3
    )

    shard = lax.axis_index("dp") * (expert_in.shape[2] // lax.axis_size("dp"))
    width = expert_in.shape[2] // lax.axis_size("dp")
    in_part = lax.dynamic_slice_in_dim(expert_in, shard, width, 2)
    out_part = lax.dynamic_slice_in_dim(expert_out, shard, width, 1)
    part_pre = jnp.einsum("erd,edf->erf", rows_all, in_part, preferred_element_type=jnp.float32)
    part_active = to_half(smooth_act(part_pre))
    part_d_active = jnp.einsum(
        "erd,efd->erf", grad_rows_all, out_part, preferred_element_type=jnp.float32
    )
    part_d_pre = to_half(part_d_active * smooth_slope(part_pre))
    grad_ein = jnp.einsum("erd,erf->edf", rows_all, part_d_pre, preferred_element_type=jnp.float32)
    grad_eout = jnp.einsum(
        "erf,erd->efd", part_active, grad_rows_all, preferred_element_type=jnp.float32
    )

    everyone = ("dp", "ctx", "exp")
    my_table_grad = jnp.dot(bucket_picks, (bias_one + bias_two).T, precision=highest)
    table_grad = lax.dynamic_update_slice(
        jnp.zeros((bucket_count, head_count), jnp.float32),
        my_table_grad,
        (0, my_group * plan.heads),
    ).reshape(bucket_count * head_count)
    attn = lax.psum_scatter(
        jnp.concatenate([attn_one, attn_two]), everyone, scatter_dimension=2, tiled=True
    ).astype(jnp.float32)
    gains = lax.psum_scatter(
        jnp.stack([gains_one[0], gains_two, gains_three[0], gains_four]),
        everyone,
        scatter_dimension=1,
        tiled=True,
    )
    table = lax.psum_scatter(table_grad, everyone, scatter_dimension=0, tiled=True)
    din = lax.psum_scatter(to_half(grad_din), everyone, scatter_dimension=1, tiled=True)
    dout = lax.psum_scatter(to_half(grad_dout), everyone, scatter_dimension=0, tiled=True)
    return (
        output,
        input_grad,
        attn[0::4],
        attn[1::4],
        attn[2::4],
        attn[3::4],
        gains,
        table,
        din.astype(jnp.float32),
        dout.astype(jnp.float32),
        grad_ein,
        grad_eout,
    )


def solution(mesh):
    in_specs = (
        P(("dp", "ctx", "exp"), None),
        P(),
        P(),
        P(),
        P(),
        P(),
        P(),
        P(),
        P(),
        P(("ctx", "exp"), None, None),
        P(("ctx", "exp"), None, None),
        P(("dp", "ctx", "exp"), None),
        P(("dp", "ctx", "exp"), None),
        P(),
        P(("dp", "ctx", "exp"), None),
    )
    out_specs = (
        P(("dp", "ctx", "exp"), None),
        P(("dp", "ctx", "exp"), None),
        P(None, None, ("dp", "ctx", "exp")),
        P(None, None, ("dp", "ctx", "exp")),
        P(None, None, ("dp", "ctx", "exp")),
        P(None, None, ("dp", "ctx", "exp")),
        P(None, ("dp", "ctx", "exp")),
        P(("dp", "ctx", "exp")),
        P(None, ("dp", "ctx", "exp")),
        P(("dp", "ctx", "exp"), None),
        P(("ctx", "exp"), None, "dp"),
        P(("ctx", "exp"), "dp", None),
    )
    return jax.shard_map(body, mesh=mesh, in_specs=in_specs, out_specs=out_specs, check_vma=False)
```

time: 2230 us -> 592 us (0.27)
  local copies, waits for them, and re-layouts: 1190 us -> 40.7 us
  waiting for transfers between devices: 707 us -> 190 us
  Pallas kernels: 0 us -> 144 us
  matrix products: 156 us -> 63.9 us
  starting transfers between devices: 13.7 us -> 38.8 us
  other arithmetic: 41 us -> 18.7 us
    gather x4 -> x0, local copies, waits for them, and re-layouts: 944 us -> none  [bias_block(): return window[:, offsets]]
    reduce_scatter x4 -> x3, waiting for transfers between devices: 600 us -> 171 us  [the longest x1 139 us: body(): lax.psum_scatter(jnp.concatenate([attn_one, attn_two]), everyone, scatter...]
    pallas_call x0 -> x4, Pallas kernels: none -> 144 us  [the longest x2 80.8 us: attention_backward(): pl.pallas_call(functools.partial(backward_kernel, plan, layer), out_shape...]
    rev x2 -> x0, local copies, waits for them, and re-layouts: 97 us -> none  [add_diagonals(): flipped = d_scores[:, ::-1, :]]
    dot_general x44 -> x6, matrix products: 125 us -> 31.9 us  [the longest x1 11.2 us: body(): jnp.einsum('erf,edf->erd', d_pre, expert_in, preferred_element_type=jnp.f...]
    unnamed x14 -> x3, waiting for transfers between devices: 50.4 us -> 0.05 us
    all_gather x8 -> x0, waiting for transfers between devices: 47.5 us -> none  [the longest x2 25.7 us: attention_forward(): lax.all_gather(values_local, ('ctx', 'exp'), axis=0, tiled=True)]
    all_gather x4 -> x0, blocking collectives: 37.2 us -> none  [the longest x2 19.1 us: attention_backward(): lax.all_gather(row_delta, ('ctx', 'exp'), axis=1, tiled=True)]
  transfers between devices with their start and end apart: 16 -> 12, of which waited for: 8 -> 6; matrix products, arithmetic and copies ran while one was open for 58% -> 11% of each run, Pallas kernels for 0% -> 7%
where the time goes in v1:
time: 592 us; the launch traced here: 583 us
  waiting for transfers between devices  190 us (32%)
  Pallas kernels  144 us (24%)
  blocking collectives  72.8 us (12%)
  matrix products  63.9 us (11%)
  local copies, waits for them, and re-layouts  40.7 us (7%)
  starting transfers between devices  38.8 us (7%)
  other arithmetic  18.7 us (3%)
  between operations  14.8 us (2%)
    reduce_scatter x1, waiting for transfers between devices, body(): lax.psum_scatter(jnp.concatenate([attn_one, attn_two]), everyone, scatter...  139 us
    pallas_call x2, Pallas kernels, attention_backward(): pl.pallas_call(functools.partial(backward_kernel, plan, layer), out_shape...  80.8 us
    pallas_call x2, Pallas kernels, attention_forward(): pl.pallas_call(functools.partial(forward_kernel, plan, layer), out_shape=...  63.2 us
    unnamed x1, blocking collectives  62 us
    reduce_scatter x1, waiting for transfers between devices, body(): lax.psum_scatter(to_half(grad_dout), everyone, scatter_dimension=0, tiled...  31.5 us
    ppermute x6, starting transfers between devices, along_dp(): lax.ppermute(values, 'dp', [(i, i ^ step) for i in range(count)])  27.8 us
    all_to_all x2, waiting for transfers between devices, to_owners(): lax.all_to_all(to_half(placed).reshape(cycle_size, local_experts, capacit...  14.2 us
    concatenate x1, local copies, waits for them, and re-layouts, body(): jnp.concatenate([attn_one, attn_two])  13.2 us
  transfers between devices with their start and end apart: 12, of which 6 were waited for; matrix products, arithmetic and copies ran while one was open for 11% of the time, Pallas kernels for 7%

profile of v1, /device:TPU:0, one launch (start us, length us, event | category | flops | bytes accessed | tf_op | source)
XLA Modules:
  0.0 583.2 jit_solution(14243396299517474056)
XLA Ops:
  7.2 0.8 slice.33
  8.0 1.2 slice.32
  9.3 0.8 slice_reduce_fusion
  10.1 0.7 pad_add_fusion
  10.9 0.8 fusion.23.bias_ref
  11.7 32.7 %attention_forward.2 = (f32[128,768]{1,0:T(8,128)}, bf16[128,768]{1,0:T(8,128)(2,1)}, bf16[4,128,256]{2,1,0:T(8,128)(2,1)}, bf16[8,128,384]{2,1,0:T(8,128)(2,1)}...) custom-call(f32[128,768]{1,0:T(8,128)} %x_ref.3, f32[4,768]{1,0:T(4,128)} %gain_ref.7, ...), custom_call_target="tpu_custom_call" | custom-call | tf_op jit(solution)/shard_map/attention_forward/pallas_call | solution.py:274
  44.4 1.1 multiply_reduce_fusion.5
  46.0 2.0 fusion.51
  48.0 1.1 copy-done.9
  49.2 1.8 convolution_add_fusion.x_ref
  50.9 30.5 %attention_forward.3 = (f32[128,768]{1,0:T(8,128)}, bf16[128,768]{1,0:T(8,128)(2,1)}, bf16[4,128,256]{2,1,0:T(8,128)(2,1)}, bf16[8,128,384]{2,1,0:T(8,128)(2,1)}...) custom-call(f32[128,768]{1,0:T(8,128)} %convolution_add_fusion.x_ref, ...), custom_call_target="tpu_custom_call" | custom-call | tf_op jit(solution)/shard_map/attention_forward/pallas_call | solution.py:274
  81.4 1.1 multiply_reduce_fusion.4
  83.6 2.1 convolution_convert_fusion.3
  85.6 3.5 all-to-all-start
  89.1 1.1 convolution_convert_fusion.2
  90.2 7.2 %all-to-all-done = bf16[8,2,16,768]{3,2,1,0:T(8,128)(2,1)S(1)} async-done(((bf16[8,2,16,768]{3,2,1,0:T(8,128)(2,1)}), bf16[8,2,16,768]{3,2,1,0:T(8,128)(2,1)S(1)}, u32[]{:S(2)}, u32[]{:S(2)}) %all-to-all-start) | async-done | bytes 393248 | tf_op jit(solution)/shard_map/all_to_all | solution.py:627
  97.4 3.5 all-to-all-start.2
  101.4 0.8 copy.58
  102.2 7.0 %all-to-all-done.2 = bf16[8,2,16,768]{3,2,1,0:T(8,128)(2,1)S(1)} async-done(((bf16[8,2,16,768]{3,2,1,0:T(8,128)(2,1)}), bf16[8,2,16,768]{3,2,1,0:T(8,128)(2,1)S(1)}, u32[]{:S(2)}, u32[]{:S(2)}) %all-to-all-start.2) | async-done | bytes 393248 | tf_op jit(solution)/shard_map/all_to_all | solution.py:627
  109.1 0.8 copy.62
  109.9 5.2 fusion.52
  115.2 11.2 %fusion.19 = bf16[1,2,128,768]{3,2,1,0:T(8,128)(2,1)} fusion(bf16[2,768,3072]{2,1,0:T(8,128)(2,1)} %param.24, bf16[2,128,768]{2,1,0:T(8,128)(2,1)} %bitcast.56, bf16[2,3072,768]{2,1,0:T(8,128)(2,1)} %param.25, f32[2,128,3072]{2,1,0:T(8,128)S(1)} %fusion.52), kind=kOutput, calls=%fused_computation.31 | convolution fusion | flops 2423193600 | bytes 22806528 | tf_op jit(solution)/shard_map/erf,edf->erd/dot_general | solution.py:674
  126.4 1.5 copy.63
  127.8 10.7 %all_to_all.60 = bf16[1,2,128,768]{3,1,0,2:T(2,128)(2,1)S(1)} all-to-all(bf16[1,2,128,768]{3,1,0,2:T(2,128)(2,1)S(1)} %copy.63), channel_id=1, replica_groups=mesh['dp'=4,'ctx'=2,'exp'=4] {'ctx','exp'}, dimensions={2} | all-to-all | bytes 786432 | tf_op jit(solution)/shard_map/all_to_all | solution.py:636
  139.1 0.9 subtract_add_fusion.1.grad_ref
  140.0 39.7 %attention_backward.2 = (f32[128,768]{1,0:T(8,128)}, f32[1,768]{1,0:T(1,128)}, bf16[4,768,768]{2,1,0:T(8,128)(2,1)}, f32[3,2048]{1,0:T(4,128)}) custom-call(f32[128,768]{1,0:T(8,128)} %subtract_add_fusion.1.grad_ref, f32[128,768]{1,0:T(8,128)} %convolution_add_fusion.x_ref, f32[4,768]{1,0:T(4,128)} %gain_ref.7, f32[3,2048]{1,0:T(4,128)} %fusion.23.bias_ref, ...), custom_call_target="tpu_custom_call" | custom-call | tf_op jit(solution)/shard_map/attention_backward/pallas_call | solution.py:516
  179.7 4.6 fusion.1
  184.4 0.9 copy-done.6
  185.3 3.7 convolution_convert_fusion.1
  189.0 5.1 convolution_convert_fusion
  194.2 0.6 copy-done.14
  194.8 4.5 multiply_reduce_fusion.1
  199.4 0.9 subtract_add_fusion.grad_ref
  200.3 41.1 %attention_backward.3 = (f32[128,768]{1,0:T(8,128)}, f32[1,768]{1,0:T(1,128)}, bf16[4,768,768]{2,1,0:T(8,128)(2,1)}, f32[3,2048]{1,0:T(4,128)}) custom-call(f32[128,768]{1,0:T(8,128)} %subtract_add_fusion.grad_ref, f32[128,768]{1,0:T(8,128)} %x_ref.3, f32[4,768]{1,0:T(4,128)} %gain_ref.7, f32[3,2048]{1,0:T(4,128)} %fusion.23.bias_ref, ...), custom_call_target="tpu_custom_call" | custom-call | tf_op jit(solution)/shard_map/attention_backward/pallas_call | solution.py:516
  241.3 9.1 %pad_maximum_fusion = bf16[8,768,768]{2,1,0:T(8,128)(2,1)} fusion(bf16[4,768,768]{2,1,0:T(8,128)(2,1)} %get-tuple-element.51, bf16[4,768,768]{2,1,0:T(8,128)(2,1)} %get-tuple-element.50), kind=kLoop, calls=%fused_computation | loop fusion | flops 4718592 | bytes 18874368 | tf_op jit(solution)/shard_map/concatenate | solution.py:717
  250.4 13.2 %copy.66 = bf16[8,768,768]{1,0,2:T(8,128)(2,1)} copy(bf16[8,768,768]{2,1,0:T(8,128)(2,1)} %pad_maximum_fusion) | data formatting | bytes 18874368 | tf_op jit(solution)/shard_map/concatenate | solution.py:717
  263.6 5.5 fusion.21
  269.3 1.2 copy.59
  270.4 3.5 all-to-all-start.1
  273.9 3.7 collective-permute-start.2
  277.7 0.7 collective-permute-start
  278.4 3.7 collective-permute-start.5
  282.4 1.0 fusion.20
  283.7 4.7 collective-permute-done.2
  288.3 19.7 %collective-permute-start.3 = (bf16[2,128,768]{2,1,0:T(8,128)(2,1)S(1)}, bf16[2,128,768]{2,1,0:T(8,128)(2,1)S(1)}, u32[]{:S(2)}, u32[]{:S(2)}) collective-permute-start(bf16[2,128,768]{2,1,0:T(8,128)(2,1)S(1)} %bitcast.59), channel_id=1, source_target_pairs={{0,8},{8,0},{16,24},{24,16},{1,9},{9,1},{17,25},{25,17},{2,10},{10... | collective-permute-start | bytes 1179656 | tf_op jit(solution)/shard_map/ppermute | solution.py:576
  308.4 62.0 %all-reduce.2 = (f32[4,768]{1,0:T(4,128)S(1)}, f32[384]{0:T(512)S(1)}) all-reduce(f32[4,768]{1,0:T(4,128)S(1)} %pad_maximum_fusion.8, f32[384]{0:T(512)S(1)} %reshape.108), channel_id=3, replica_groups=mesh['dp'=4,'ctx'=2,'exp'=4] {'dp','ctx','exp'}, use_global_device_ids=true, to_apply=%region_9.10.clone | all-reduce | flops 3456 | bytes 27648
  371.0 0.6 constant_dynamic-slice_fusion
  371.7 3.1 fusion.2
  374.8 1.6 copy-done.32
  376.4 4.9 fusion.8
  381.3 6.7 %fusion.12 = f32[2,768,768]{2,1,0:T(8,128)} fusion(f32[2,512,768]{2,1,0:T(8,128)} %copy-done.32, bf16[2,3072,768]{2,1,0:T(8,128)(2,1)} %param.25, s32[]{:T(128)S(6)} %select_n.15, bf16[2,128,768]{2,1,0:T(8,128)(2,1)} %collective-permute-done.5, bf16[2,128,768]{2,1,0:T(8,128)(2,1)} %collective-permute-done.4, ...), kind=kOutput, calls=%fused_computation.26 | convolution fusion | flops 2435579904 | bytes 13369348 | tf_op jit(solution)/shard_map/erd,erf->edf/dot_general | solution.py:704
  388.0 1.7 convert_element_type.77
  389.7 31.5 %reduce-scatter.9.cloned.1.call-done = bf16[96,768]{1,0:T(8,128)(2,1)} async-done(((bf16[3072,768]{1,0:T(8,128)(2,1)}), bf16[96,768]{1,0:T(8,128)(2,1)}) %reduce-scatter.9.cloned.1.call-update) | async-done | bytes 147472 | tf_op jit(solution)/shard_map/reduce_scatter | solution.py:727
  421.2 1.6 convert_element_type.79
  422.9 139.0 %reduce-scatter.5.cloned.1.call-done = bf16[8,768,24]{1,0,2:T(8,128)(2,1)} async-done(((bf16[8,768,768]{1,0,2:T(8,128)(2,1)}), bf16[8,768,24]{1,0,2:T(8,128)(2,1)}) %reduce-scatter.5.cloned.1.call-update) | async-done | bytes 294928 | tf_op jit(solution)/shard_map/reduce_scatter | solution.py:716
  561.9 2.7 slice.37
  564.6 0.7 copy.70
  565.3 2.7 slice.38
  568.0 0.7 copy.71
  568.7 2.7 slice.39
  571.4 0.7 copy.72
  572.1 2.7 slice.40
  574.8 0.7 copy.73
  575.4 0.7 copy.81
  (105 shorter events, 4.4 us)
Async XLA Ops:
  7.2 3.7 copy-start
  9.3 36.7 %slice-start = ((s8[4718592]{0:T(1024)(128)(4,1)}), s8[524288]{0:T(1024)(128)(4,1)S(1)}, s32[]{:S(2)}) async-start(s8[4718592]{0:T(1024)(128)(4,1)} %bitcast.42), calls=%async_computation.10 | async-start | bytes 1048576
  10.9 33.5 %copy-start.18 = (s32[2048]{0:T(1024)}, s32[2048]{0:T(1024)S(1)}, u32[]{:S(2)}) copy-start(s32[2048]{0:T(1024)S(1)} %pad_add_fusion) | copy-start | bytes 24580
  11.7 34.3 %slice-start.1 = ((s8[4718592]{0:T(1024)(128)(4,1)}), s8[4194304]{0:T(1024)(128)(4,1)S(1)}, s32[]{:S(2)}) async-start(s8[4718592]{0:T(1024)(128)(4,1)} %bitcast.42), calls=%async_computation.11 | async-start | bytes 8388608
  46.0 138.4 %copy-start.13 = (f32[128]{0:T(128)}, f32[128]{0:T(128)S(1)}, u32[]{:S(2)}) copy-start(f32[128]{0:T(128)S(1)} %get-tuple-element.113) | copy-start | bytes 1540
  46.0 3.2 copy-start.2
  46.0 3.1 copy-start.29
  48.0 1.1 copy-start.9
  50.9 32.1 %copy-start.24 = (s32[128,1]{0,1:T(1,128)S(1)}, s32[128,1]{0,1:T(1,128)}, u32[]{:S(2)}) copy-start(s32[128,1]{0,1:T(1,128)} %param.26) | copy-start | bytes 1540
  50.9 38.1 %copy-start.7 = (f32[128,768]{1,0:T(8,128)S(1)}, f32[128,768]{1,0:T(8,128)}, u32[]{:S(2)}) copy-start(f32[128,768]{1,0:T(8,128)} %param.29) | copy-start | bytes 1179652
  50.9 38.2 %copy-start.25 = (f32[128,1]{0,1:T(1,128)S(1)}, f32[128,1]{0,1:T(1,128)}, u32[]{:S(2)}) copy-start(f32[128,1]{0,1:T(1,128)} %param.27) | copy-start | bytes 1540
  83.1 2.5 copy-start.20
  83.5 31.6 %copy-start.15 = (s32[128]{0:T(128)}, s32[128]{0:T(128)S(1)}, u32[]{:S(2)}) copy-start(s32[128]{0:T(128)S(1)} %multiply_add_fusion) | copy-start | bytes 1540
  85.6 11.8 %all-to-all-start = ((bf16[8,2,16,768]{3,2,1,0:T(8,128)(2,1)}), bf16[8,2,16,768]{3,2,1,0:T(8,128)(2,1)S(1)}, u32[]{:S(2)}, u32[]{:S(2)}) async-start(bf16[8,2,16,768]{3,2,1,0:T(8,128)(2,1)} %bitcast.2), calls=%async_computation | async-start | bytes 786432 | tf_op jit(solution)/shard_map/all_to_all | solution.py:627
  97.4 11.7 %all-to-all-start.2 = ((bf16[8,2,16,768]{3,2,1,0:T(8,128)(2,1)}), bf16[8,2,16,768]{3,2,1,0:T(8,128)(2,1)S(1)}, u32[]{:S(2)}, u32[]{:S(2)}) async-start(bf16[8,2,16,768]{3,2,1,0:T(8,128)(2,1)} %bitcast.10), calls=%async_computation.2 | async-start | bytes 786432 | tf_op jit(solution)/shard_map/all_to_all | solution.py:627
  100.9 287.1 %reduce-scatter.7.cloned.1.call-start = ((), (), s32[]{:S(2)}) async-start(), calls=%async_computation.8 | async-start | bytes 4866048 | tf_op jit(solution)/shard_map/reduce_scatter | solution.py:726
  126.3 12.3 %copy-start.3 = (f32[128,768]{1,0:T(8,128)S(1)}, f32[128,768]{1,0:T(8,128)}, u32[]{:S(2)}) copy-start(f32[128,768]{1,0:T(8,128)} %get-tuple-element.35) | copy-start | bytes 1179652
  126.3 12.3 %copy-start.16 = (s32[128]{0:T(128)S(1)}, s32[128]{0:T(128)}, u32[]{:S(2)}) copy-start(s32[128]{0:T(128)} %copy-done.15) | copy-start | bytes 1540
  126.3 12.3 %copy-start.21 = (f32[128]{0:T(128)S(1)}, f32[128]{0:T(128)}, u32[]{:S(2)}) copy-start(f32[128]{0:T(128)} %copy-done.20) | copy-start | bytes 1540
  126.3 12.7 %copy-start.8 = (f32[128,768]{1,0:T(8,128)S(1)}, f32[128,768]{1,0:T(8,128)}, u32[]{:S(2)}) copy-start(f32[128,768]{1,0:T(8,128)} %param.29) | copy-start | bytes 1179652
  126.4 12.7 %copy-start.28 = (f32[128]{0:T(128)S(1)}, f32[128]{0:T(128)}, u32[]{:S(2)}) copy-start(f32[128]{0:T(128)} %get-tuple-element.114) | copy-start | bytes 1540
  184.4 0.9 copy-start.6
  189.0 232.2 %reduce-scatter.9.cloned.1.call-start = ((), (), s32[]{:S(2)}) async-start(), calls=%async_computation.9 | async-start | bytes 4866048 | tf_op jit(solution)/shard_map/reduce_scatter | solution.py:727
  194.2 0.7 copy-start.14
  194.2 367.7 %reduce-scatter.5.cloned.1.call-start = ((), (), s32[]{:S(2)}) async-start(), calls=%async_computation.7 | async-start | bytes 9732096 | tf_op jit(solution)/shard_map/reduce_scatter | solution.py:716
  194.8 4.5 copy-start.12
  194.8 4.5 copy-start.27
  263.6 10.3 %copy-start.5 = (bf16[1,2,8,16,768]{4,3,2,1,0:T(8,128)(2,1)S(1)}, bf16[1,2,8,16,768]{4,3,2,1,0:T(8,128)(2,1)}, u32[]{:S(2)}) copy-start(bf16[1,2,8,16,768]{4,3,2,1,0:T(8,128)(2,1)} %copy.58) | copy-start | bytes 1179652
  269.2 13.2 %copy-start.4 = (f32[128,768]{1,0:T(8,128)S(1)}, f32[128,768]{1,0:T(8,128)}, u32[]{:S(2)}) copy-start(f32[128,768]{1,0:T(8,128)} %get-tuple-element.35) | copy-start | bytes 1179652
  269.2 13.2 %copy-start.17 = (s32[128]{0:T(128)S(1)}, s32[128]{0:T(128)}, u32[]{:S(2)}) copy-start(s32[128]{0:T(128)} %copy-done.15) | copy-start | bytes 1540
  269.2 13.2 %copy-start.26 = (f32[128,1]{0,1:T(1,128)S(1)}, f32[128,1]{0,1:T(1,128)}, u32[]{:S(2)}) copy-start(f32[128,1]{0,1:T(1,128)} %param.27) | copy-start | bytes 1540
  269.2 14.2 %copy-start.19 = (s32[2048]{0:T(1024)S(1)}, s32[2048]{0:T(1024)}, u32[]{:S(2)}) copy-start(s32[2048]{0:T(1024)} %copy-done.18) | copy-start | bytes 24580
  269.2 14.2 %copy-start.30 = (f32[3,2048]{1,0:T(4,128)S(1)}, f32[3,2048]{1,0:T(4,128)}, u32[]{:S(2)}) copy-start(f32[3,2048]{1,0:T(4,128)} %get-tuple-element.55) | copy-start | bytes 73732
  269.2 14.2 %copy-start.31 = (f32[3,2048]{1,0:T(4,128)S(1)}, f32[3,2048]{1,0:T(4,128)}, u32[]{:S(2)}) copy-start(f32[3,2048]{1,0:T(4,128)} %get-tuple-element.54) | copy-start | bytes 73732
  269.2 19.1 %copy-start.10 = (bf16[1,2,8,16,768]{4,3,2,1,0:T(8,128)(2,1)S(1)}, bf16[1,2,8,16,768]{4,3,2,1,0:T(8,128)(2,1)}, u32[]{:S(2)}) copy-start(bf16[1,2,8,16,768]{4,3,2,1,0:T(8,128)(2,1)} %copy.62) | copy-start | bytes 1179652
  269.2 38.8 %copy-start.22 = (f32[1,768]{1,0:T(1,128)S(1)}, f32[1,768]{1,0:T(1,128)}, u32[]{:S(2)}) copy-start(f32[1,768]{1,0:T(1,128)} %get-tuple-element.53) | copy-start | bytes 9220
  269.3 38.7 %copy-start.23 = (f32[1,768]{1,0:T(1,128)S(1)}, f32[1,768]{1,0:T(1,128)}, u32[]{:S(2)}) copy-start(f32[1,768]{1,0:T(1,128)} %get-tuple-element.52) | copy-start | bytes 9220
  270.4 11.9 %all-to-all-start.1 = ((bf16[1,2,128,768]{3,1,0,2:T(2,128)(2,1)}), bf16[1,2,128,768]{3,1,0,2:T(2,128)(2,1)S(1)}, u32[]{:S(2)}, u32[]{:S(2)}) async-start(bf16[1,2,128,768]{3,1,0,2:T(2,128)(2,1)} %copy.59), calls=%async_computation.1 | async-start | bytes 786432 | tf_op jit(solution)/shard_map/all_to_all | solution.py:636
  273.9 14.4 %collective-permute-start.2 = (bf16[2,128,768]{2,1,0:T(8,128)(2,1)S(1)}, bf16[2,128,768]{2,1,0:T(8,128)(2,1)S(1)}, u32[]{:S(2)}, u32[]{:S(2)}) collective-permute-start(bf16[2,128,768]{2,1,0:T(8,128)(2,1)S(1)} %bitcast.45), channel_id=1, source_target_pairs={{0,24},{8,16},{16,8},{24,0},{1,25},{9,17},{17,9},{25,1},{2,26},{10... | collective-permute-start | bytes 1179656 | tf_op jit(solution)/shard_map/ppermute | solution.py:576
  277.7 94.0 %collective-permute-start.1 = (bf16[2,128,768]{2,1,0:T(8,128)(2,1)S(1)}, bf16[2,128,768]{2,1,0:T(8,128)(2,1)S(1)}, u32[]{:S(2)}, u32[]{:S(2)}) collective-permute-start(bf16[2,128,768]{2,1,0:T(8,128)(2,1)S(1)} %bitcast.46), channel_id=1, source_target_pairs={{0,16},{8,24},{16,0},{24,8},{1,17},{9,25},{17,1},{25,9},{2,18},{10... | collective-permute-start | bytes 1179656 | tf_op jit(solution)/shard_map/ppermute | solution.py:576
  277.7 94.0 %collective-permute-start = (bf16[2,128,768]{2,1,0:T(8,128)(2,1)S(1)}, bf16[2,128,768]{2,1,0:T(8,128)(2,1)S(1)}, u32[]{:S(2)}, u32[]{:S(2)}) collective-permute-start(bf16[2,128,768]{2,1,0:T(8,128)(2,1)S(1)} %bitcast.47), channel_id=1, source_target_pairs={{0,8},{8,0},{16,24},{24,16},{1,9},{9,1},{17,25},{25,17},{2,10},{10... | collective-permute-start | bytes 1179656 | tf_op jit(solution)/shard_map/ppermute | solution.py:576
  278.4 96.3 %collective-permute-start.5 = (bf16[2,128,768]{2,1,0:T(8,128)(2,1)}, bf16[2,128,768]{2,1,0:T(8,128)(2,1)}, u32[]{:S(2)}, u32[]{:S(2)}) collective-permute-start(bf16[2,128,768]{2,1,0:T(8,128)(2,1)} %bitcast.57), channel_id=1, source_target_pairs={{0,24},{8,16},{16,8},{24,0},{1,25},{9,17},{17,9},{25,1},{2,26},{10... | collective-permute-start | bytes 1179656 | tf_op jit(solution)/shard_map/ppermute | solution.py:576
  282.1 92.7 %collective-permute-start.4 = (bf16[2,128,768]{2,1,0:T(8,128)(2,1)}, bf16[2,128,768]{2,1,0:T(8,128)(2,1)}, u32[]{:S(2)}, u32[]{:S(2)}) collective-permute-start(bf16[2,128,768]{2,1,0:T(8,128)(2,1)} %bitcast.58), channel_id=1, source_target_pairs={{0,16},{8,24},{16,0},{24,8},{1,17},{9,25},{17,1},{25,9},{2,18},{10... | collective-permute-start | bytes 1179656 | tf_op jit(solution)/shard_map/ppermute | solution.py:576
  288.3 86.4 %collective-permute-start.3 = (bf16[2,128,768]{2,1,0:T(8,128)(2,1)S(1)}, bf16[2,128,768]{2,1,0:T(8,128)(2,1)S(1)}, u32[]{:S(2)}, u32[]{:S(2)}) collective-permute-start(bf16[2,128,768]{2,1,0:T(8,128)(2,1)S(1)} %bitcast.59), channel_id=1, source_target_pairs={{0,8},{8,0},{16,24},{24,16},{1,9},{9,1},{17,25},{25,17},{2,10},{10... | collective-permute-start | bytes 1179656 | tf_op jit(solution)/shard_map/ppermute | solution.py:576
  374.7 1.7 copy-start.32
  381.3 194.9 %copy-start.1 = (f32[32,12]{0,1:T(8,128)S(1)}, f32[32,12]{0,1:T(8,128)}, u32[]{:S(2)}) copy-start(f32[32,12]{0,1:T(8,128)} %param.21) | copy-start | bytes 4612
  388.0 187.4 %copy-start.11 = (f32[128,768]{1,0:T(8,128)S(1)}, f32[128,768]{1,0:T(8,128)}, u32[]{:S(2)}) copy-start(f32[128,768]{1,0:T(8,128)} %get-tuple-element.131) | copy-start | bytes 1179652
Sparse Core Ops, SparseCore 0:
  189.1 118.3 reduce-scatter.6
  313.8 107.3 reduce-scatter.8
  427.1 134.7 reduce-scatter.4
